TPU v7x, 128 devices: a whole 4x4x4 slice. The times are simulated.
128 devices in a mesh: role: 2 (over y_lo), grp: 64 (over y_hi, z, x, core).
Axes of the slice: x: 4, y: 4 (y_hi: 2, y_lo: 2; y = y_hi * 2 + y_lo), z: 4, core: 2. Of those that a mesh axis runs over, the one named last changes fastest.
Arguments:
- hidden_state: float32 [128, 8192], P(None, ('role', 'grp')), may hold values from -6 to 6
- gain_attn: float32 [8192], P(('role', 'grp')), may hold values from 0.25 to 1.75
- gain_ffn: float32 [8192], P(('role', 'grp')), may hold values from 0.25 to 1.75
- w_qkv: bfloat16 [9216, 8192], P(('role', 'grp')), may hold values from -0.0625 to 0.0625
- w_out: bfloat16 [8192, 8192], P(('role', 'grp')), may hold values from -0.0625 to 0.0625
- w_gate: bfloat16 [53248, 8192], P(('role', 'grp')), may hold values from -0.0625 to 0.0625
- w_up: bfloat16 [53248, 8192], P(('role', 'grp')), may hold values from -0.0625 to 0.0625
- w_down: bfloat16 [53248, 8192], P(('role', 'grp')), may hold values from -0.02734375 to 0.02734375
- kv_cache: bfloat16 [128, 1024, 1024], P(('role', 'grp'))
- lengths: int32 [128], replicated, may hold values from 1 to 1024, as said below
- row_order: int32 [128], replicated, may hold values from 0 to 127, each once
Outputs:
- out_state: float32 [128, 8192], P(None, ('role', 'grp'))
Inputs may be any that keep to these rules, and one draw needn't show every extreme that they name: `lengths`: every sequence has at least one cached position; some sequence has all 1024. `row_order`: each sequence is named by exactly one cache row.
All inputs are finite; a program needn't handle non-finite values.
Results may differ from a plain program's by a relative error of at most 0.0099.
Values may be sent and summed in bfloat16 or wider, within the bound.
A program may use at most 128 MiB of HBM per device.

v0:
```python
import jax
import jax.numpy as jnp
from jax import lax
from jax.sharding import PartitionSpec as P

QH = 64
KVH = 4
HD = 128


def contract_rows(left, right):
    return lax.dot_general(
        left, right, (((1,), (1,)), ((), ())), preferred_element_type=jnp.float32
    )


def per_device(
    hidden_state,
    gain_attn,
    gain_ffn,
    w_qkv,
    w_out,
    w_gate,
    w_up,
    w_down,
    kv_cache,
    lengths,
    row_order,
):
    place = lax.axis_index("role") * lax.axis_size("grp") + lax.axis_index("grp")
    total_rows = hidden_state.shape[0]
    owned = kv_cache.shape[0]
    length = kv_cache.shape[1]
    key_width = KVH * HD
    query_width = QH * HD
    groups = QH // KVH
    scale = 1.0 / HD**0.5
    inverse = (
        jnp.zeros((total_rows,), jnp.int32)
        .at[row_order]
        .set(jnp.arange(total_rows, dtype=jnp.int32))
    )
    slot_lens = lax.dynamic_slice_in_dim(lengths[row_order], place * owned, owned)
    valid = (jnp.arange(length, dtype=jnp.int32)[None, :] < slot_lens[:, None])[:, None, None, :]
    keys = kv_cache[:, :, :key_width].reshape(owned, length, KVH, HD)
    values = kv_cache[:, :, key_width:].reshape(owned, length, KVH, HD)

    def full_normed(state, gain):
        whole, whole_gain = (
            lax.all_gather(state, ("role", "grp"), axis=1, tiled=True),
            lax.all_gather(gain, ("role", "grp"), axis=0, tiled=True),
        )
        mean = jnp.mean(whole * whole, axis=1, keepdims=True)
        return (whole * lax.rsqrt(mean + 1e-05) * whole_gain).astype(jnp.bfloat16)

    state = hidden_state
    normed_a = full_normed(state, gain_attn)
    projected = contract_rows(normed_a, w_qkv).astype(jnp.bfloat16)
    mine = lax.all_to_all(
        projected[row_order], ("role", "grp"), split_axis=0, concat_axis=1, tiled=True
    )
    recent = [mine[:, query_width:]]
    query = mine[:, :query_width]
    query = query.reshape(owned, KVH, groups, HD)
    fresh_all = jnp.stack(recent, axis=1)
    count = fresh_all.shape[1]
    new_keys = fresh_all[:, :, :key_width].reshape(owned, count, KVH, HD)
    new_values = fresh_all[:, :, key_width:].reshape(owned, count, KVH, HD)
    cached = jnp.einsum("rkgd,rlkd->rkgl", query, keys, preferred_element_type=jnp.float32) * scale
    cached = jnp.where(valid, cached, -1e30)
    fresh = (
        jnp.einsum("rkgd,rjkd->rkgj", query, new_keys, preferred_element_type=jnp.float32) * scale
    )
    top = jnp.maximum(jnp.max(cached, axis=-1), jnp.max(fresh, axis=-1))
    cached_w = jnp.where(valid, jnp.exp(cached - top[..., None]), 0.0)
    fresh_w = jnp.exp(fresh - top[..., None])
    total = jnp.sum(cached_w, axis=-1) + jnp.sum(fresh_w, axis=-1)
    summed = jnp.einsum(
        "rkgl,rlkd->rkgd", cached_w.astype(jnp.bfloat16), values, preferred_element_type=jnp.float32
    )
    summed = summed + jnp.einsum(
        "rkgj,rjkd->rkgd",
        fresh_w.astype(jnp.bfloat16),
        new_values,
        preferred_element_type=jnp.float32,
    )
    attended = (summed / total[..., None]).reshape(owned, query_width).astype(jnp.bfloat16)
    delta = contract_rows(lax.all_gather(attended, ("role", "grp"), axis=0, tiled=True), w_out)
    state = state + delta[inverse]
    normed_f = full_normed(state, gain_ffn)
    gate = contract_rows(normed_f, w_gate)
    upper = contract_rows(normed_f, w_up)
    hidden = (jax.nn.silu(gate) * upper).astype(jnp.bfloat16)
    term = jnp.dot(hidden, w_down, preferred_element_type=jnp.float32)
    summed = lax.psum_scatter(term, ("role", "grp"), scatter_dimension=1, tiled=True)
    state = state + summed
    return state


def solution(mesh):
    in_specs = (
        P(None, ("role", "grp")),
        P(("role", "grp")),
        P(("role", "grp")),
        P(("role", "grp"), None),
        P(("role", "grp"), None),
        P(("role", "grp"), None),
        P(("role", "grp"), None),
        P(("role", "grp"), None),
        P(("role", "grp"), None, None),
        P(),
        P(),
    )
    out_specs = P(None, ("role", "grp"))
    return jax.shard_map(
        per_device, mesh=mesh, in_specs=in_specs, out_specs=out_specs, check_vma=False
    )
```

profile of v0, /device:TPU:24, one launch (start us, length us, event | category | flops | bytes accessed | tf_op | source)
XLA Modules:
  0.0 1463.9 jit_solution(14356021649416771107)
XLA Ops:
  6.5 0.7 all-gather.5.cloned.1.call-update
  7.3 0.9 dynamic-update-slice
  8.2 0.9 dynamic-update-slice.1
  9.1 0.6 copy-done.7
  9.7 0.7 compare_select_fusion.1
  10.4 3.0 fusion.31
  13.4 1.2 gather_fusion
  14.6 0.7 dynamic_slice.3
  15.3 192.8 %all-gather.5.cloned.1.call-done = f32[128,8192]{0,1:T(8,128)} async-done(((f32[128,64]{0,1:T(8,128)}), f32[128,8192]{0,1:T(8,128)}) %all-gather.5.cloned.1.call-update) | async-done | bytes 4194320 | tf_op jit(solution)/shard_map/all_gather | solution.py:50
  208.1 3.3 multiply_reduce_fusion.1
  211.4 136.7 %all-reduce.5.cloned.1.call-done = (f32[8192]{0:T(1024)}, f32[8192]{0:T(1024)}) async-done(((f32[8192]{0:T(1024)}, f32[8192]{0:T(1024)}), (f32[8192]{0:T(1024)}, f32[8192]{0:T(1024)})) %all-reduce.5.cloned.1.call-update) | async-done | bytes 65552
  348.0 5.0 fusion.9
  353.1 0.7 gather_fusion.1
  353.8 0.7 copy.24
  354.5 8.2 all-to-all-start
  362.7 0.6 iota_compare_fusion
  363.4 0.5 copy.37
  363.9 1.5 copy.38
  365.4 5.6 all-to-all-done
  372.2 0.4 fusion.10
  372.6 0.6 reshape.174
  373.3 1.0 scatter_custom_fusion
  374.4 193.5 %all-gather.9.cloned.1.call-done = bf16[128,1,8192]{2,1,0:T(2,128)(2,1)} async-done(((bf16[1,1,8192]{2,1,0:T(2,128)(2,1)}), bf16[128,1,8192]{2,1,0:T(2,128)(2,1)}) %all-gather.9.cloned.1.call-update) | async-done | bytes 2097168 | tf_op jit(solution)/shard_map/all_gather | solution.py:88
  567.9 4.9 fusion.1
  572.8 0.7 gather_fusion.2
  573.5 0.6 add.60
  574.4 196.4 %all-gather.7.cloned.1.call-done = f32[128,8192]{0,1:T(8,128)} async-done(((f32[128,64]{0,1:T(8,128)}), f32[128,8192]{0,1:T(8,128)}) %all-gather.7.cloned.1.call-update) | async-done | bytes 4194320 | tf_op jit(solution)/shard_map/all_gather | solution.py:50
  770.8 3.4 multiply_reduce_fusion
  774.2 5.2 fusion.30
  779.5 15.9 %fusion.11 = f32[128,8192]{0,1:T(8,128)} fusion(bf16[416,8192]{1,0:T(8,128)(2,1)} %param.18, bf16[416,8192]{1,0:T(8,128)(2,1)} %param.17, f32[128,416]{0,1:T(8,128)S(1)} %fusion.30, f32[128,8192]{0,1:T(8,128)} %all-gather.7.cloned.1.call-done, f32[8192]{0:T(1024)S(1)} %copy-done.5, f32[128]{0:T(128)S(1)} %add_rsqrt_fusion), kind=kOutput, calls=%fused_computation.22 | convolution fusion | flops 1748295680 | bytes 22266368 | tf_op jit(solution)/shard_map/dot_general | solution.py:94
  795.4 660.6 %reduce-scatter.2.cloned.1.call-done = f32[128,64]{0,1:T(8,128)} async-done(((f32[128,8192]{0,1:T(8,128)}), f32[128,64]{0,1:T(8,128)}) %reduce-scatter.2.cloned.1.call-update) | async-done | bytes 32784 | tf_op jit(solution)/shard_map/reduce_scatter | solution.py:95
  1456.0 1.4 add.63
  (46 shorter events, 1.8 us)
Async XLA Ops:
  6.5 341.5 %copy-start = (bf16[72,8192]{1,0:T(8,128)(2,1)S(1)}, bf16[72,8192]{1,0:T(8,128)(2,1)}, u32[]{:S(2)}) copy-start(bf16[72,8192]{1,0:T(8,128)(2,1)} %param.14) | copy-start | bytes 3538948
  6.5 6.8 copy-start.1
  6.5 201.5 %all-gather.5.cloned.1.call-start = ((), (), s32[]{:S(2)}) async-start(), calls=%async_computation.2 | async-start | bytes 4227072 | tf_op jit(solution)/shard_map/all_gather | solution.py:50
  7.3 340.8 %all-reduce.5.cloned.1.call-start = ((), (), s32[]{:S(2)}) async-start(), calls=%async_computation.6 | async-start | bytes 131072
  8.2 0.9 copy-start.8
  9.1 0.6 copy-start.7
  15.3 348.1 %copy-start.3 = (bf16[1,1024,512]{2,1,0:T(8,128)(2,1)S(1)}, bf16[1,1024,512]{2,1,0:T(8,128)(2,1)}, u32[]{:S(2)}) copy-start(bf16[1,1024,512]{2,1,0:T(8,128)(2,1)} %get-tuple-element.7) | copy-start | bytes 3145732
  354.5 16.6 %all-to-all-start = ((bf16[128,1,72]{2,1,0:T(2,128)(2,1)}), bf16[128,1,72]{2,1,0:T(2,128)(2,1)S(1)}, u32[]{:S(2)}, u32[]{:S(2)}) async-start(bf16[128,1,72]{2,1,0:T(2,128)(2,1)} %copy.24), calls=%async_computation | async-start | bytes 131072 | tf_op jit(solution)/shard_map/all_to_all | solution.py:59
  362.7 205.2 %all-gather.9.cloned.1.call-start = ((), (), s32[]{:S(2)}) async-start(), calls=%async_computation.5 | async-start | bytes 4227072 | tf_op jit(solution)/shard_map/all_gather | solution.py:88
  365.4 208.1 %copy-start.6 = (f32[128,64]{0,1:T(8,128)S(1)}, f32[128,64]{0,1:T(8,128)}, u32[]{:S(2)}) copy-start(f32[128,64]{0,1:T(8,128)} %param.11) | copy-start | bytes 98308
  373.3 397.5 %all-gather.7.cloned.1.call-start = ((), (), s32[]{:S(2)}) async-start(), calls=%async_computation.3 | async-start | bytes 4227072 | tf_op jit(solution)/shard_map/all_gather | solution.py:50
  374.4 399.8 %copy-start.5 = (f32[8192]{0:T(1024)S(1)}, f32[8192]{0:T(1024)}, u32[]{:S(2)}) copy-start(f32[8192]{0:T(1024)} %get-tuple-element.6) | copy-start | bytes 98308
  574.2 881.9 %reduce-scatter.2.cloned.1.call-start = ((), (), s32[]{:S(2)}) async-start(), calls=%async_computation.4 | async-start | bytes 4227072 | tf_op jit(solution)/shard_map/reduce_scatter | solution.py:95
  770.8 3.4 copy-start.2
  795.4 660.7 %copy-start.4 = (f32[128,64]{0,1:T(8,128)S(1)}, f32[128,64]{0,1:T(8,128)}, u32[]{:S(2)}) copy-start(f32[128,64]{0,1:T(8,128)} %add.60) | copy-start | bytes 98308
Sparse Core Ops, SparseCore 0:
  9.1 198.9 all-gather.4
  213.1 134.9 all-reduce.4
  373.4 194.4 all-gather.8
  574.3 196.4 all-gather.6
  795.5 660.4 reduce-scatter.1
where the time goes:
time: 1460 us
  waiting for transfers between devices  1390 us (95%)
  matrix products  31.9 us (2%)
    reduce_scatter x1, waiting for transfers between devices, per_device(): lax.psum_scatter(term, ('role', 'grp'), scatter_dimension=1, tiled=True)  661 us
    all_gather x2, waiting for transfers between devices, full_normed(): lax.all_gather(state, ('role', 'grp'), axis=1, tiled=True)  389 us
    all_gather x1, waiting for transfers between devices, per_device(): lax.all_gather(attended, ('role', 'grp'), axis=0, tiled=True)  194 us
    unnamed x6, waiting for transfers between devices  137 us
  transfers between devices with their start and end apart: 6, of which 6 were waited for; matrix products, arithmetic and copies ran while one was open for 1% of the time, Pallas kernels for 0%

commit v1 on v0

--- a/solution.py
+++ b/solution.py
@@ -1,3 +1,4 @@
+import functools
 import jax
 import jax.numpy as jnp
 from jax import lax
@@ -6,6 +7,15 @@
 QH = 64
 KVH = 4
 HD = 128
+
+
+def obtain_seats_all_over_axis(matrix, mesh_dim, axis_k):
+    g_now = lax.all_to_all(jnp.stack(lax.axis_size(mesh_dim) * [matrix]), mesh_dim, 0, 0)
+    current_value = jnp.concatenate(g_now, axis=axis_k)
+    return current_value
+
+
+map_pairs_all = functools.partial(obtain_seats_all_over_axis, mesh_dim=("role", "grp"), axis_k=1)
 
 
 def contract_rows(left, right):
@@ -47,7 +57,7 @@
 
     def full_normed(state, gain):
         whole, whole_gain = (
-            lax.all_gather(state, ("role", "grp"), axis=1, tiled=True),
+            map_pairs_all(state),
             lax.all_gather(gain, ("role", "grp"), axis=0, tiled=True),
         )
         mean = jnp.mean(whole * whole, axis=1, keepdims=True)

time: 1460 us -> 1170 us (0.80)
  waiting for transfers between devices: 1390 us -> 1020 us
  blocking collectives: 0 us -> 59.6 us
    all_gather x2 -> x0, waiting for transfers between devices: 389 us -> none  [full_normed(): lax.all_gather(state, ('role', 'grp'), axis=1, tiled=True)]
    all_to_all x0 -> x1, blocking collectives: none -> 59.6 us  [obtain_seats_all_over_axis(): lax.all_to_all(jnp.stack(lax.axis_size(mesh_dim) * [matrix]), mesh_dim, 0...]
    all_to_all x0 -> x1, waiting for transfers between devices: none -> 45.9 us  [obtain_seats_all_over_axis(): lax.all_to_all(jnp.stack(lax.axis_size(mesh_dim) * [matrix]), mesh_dim, 0...]
    unnamed x6 -> x4, waiting for transfers between devices: 137 us -> 115 us
  transfers between devices with their start and end apart: 6 -> 5, of which waited for: 6 -> 5; matrix products, arithmetic and copies ran while one was open for 1% -> 1% of each run, Pallas kernels for 0% -> 0%
where the time goes in v1:
time: 1170 us
  waiting for transfers between devices  1020 us (87%)
  blocking collectives  59.6 us (5%)
  matrix products  22.7 us (2%)
  starting transfers between devices  19 us (2%)
  local copies, waits for them, and re-layouts  15.8 us (1%)
  between operations  13.4 us (1%)
  other arithmetic  13.3 us (1%)
    reduce_scatter x1, waiting for transfers between devices, per_device(): lax.psum_scatter(term, ('role', 'grp'), scatter_dimension=1, tiled=True)  661 us
    all_gather x1, waiting for transfers between devices, per_device(): lax.all_gather(attended, ('role', 'grp'), axis=0, tiled=True)  194 us
    unnamed x4, waiting for transfers between devices  115 us
    all_to_all x1, blocking collectives, obtain_seats_all_over_axis(): lax.all_to_all(jnp.stack(lax.axis_size(mesh_dim) * [matrix]), mesh_dim, 0...  59.6 us
    all_to_all x1, waiting for transfers between devices, obtain_seats_all_over_axis(): lax.all_to_all(jnp.stack(lax.axis_size(mesh_dim) * [matrix]), mesh_dim, 0...  45.9 us
  transfers between devices with their start and end apart: 5, of which 5 were waited for; matrix products, arithmetic and copies ran while one was open for 1% of the time, Pallas kernels for 0%

profile of v1, /device:TPU:24, one launch (start us, length us, event | category | flops | bytes accessed | tf_op | source)
XLA Modules:
  0.0 1165.4 jit_solution(2149223802316327265)
XLA Ops:
  6.5 3.4 stack.6
  9.9 10.7 all-to-all-start
  22.0 1.2 gather_fusion
  23.2 0.7 dynamic_slice.3
  23.9 2.7 fusion.32
  26.6 45.9 %all-to-all-done = f32[128,128,64]{1,2,0:T(8,128)} async-done(((f32[128,128,64]{1,2,0:T(8,128)}), f32[128,128,64]{1,2,0:T(8,128)}, u32[]{:S(2)}, u32[]{:S(2)}) %all-to-all-start) | async-done | bytes 4194336 | tf_op jit(solution)/shard_map/all_to_all | solution.py:13
  72.4 3.3 fusion.5
  75.7 115.1 %all-reduce.5.cloned.1.call-done = (f32[8192]{0:T(1024)}, f32[8192]{0:T(1024)}) async-done(((f32[8192]{0:T(1024)}, f32[8192]{0:T(1024)}), (f32[8192]{0:T(1024)}, f32[8192]{0:T(1024)})) %all-reduce.5.cloned.1.call-update) | async-done | bytes 65552
  190.8 2.9 fusion.3
  193.7 0.5 convolution_convert_fusion
  194.3 0.7 gather_fusion.1
  195.1 0.7 copy.26
  195.7 8.2 all-to-all-start.1
  204.0 0.7 iota_compare_fusion
  204.7 0.5 copy.39
  205.2 1.5 copy.40
  206.7 5.6 all-to-all-done.1
  212.9 0.3 fusion.33
  213.4 0.4 fusion.12
  213.8 0.6 reshape.194
  214.6 1.0 scatter_custom_fusion
  215.6 193.5 %all-gather.3.cloned.1.call-done = bf16[128,1,8192]{2,1,0:T(2,128)(2,1)} async-done(((bf16[1,1,8192]{2,1,0:T(2,128)(2,1)}), bf16[128,1,8192]{2,1,0:T(2,128)(2,1)}) %all-gather.3.cloned.1.call-update) | async-done | bytes 2097168 | tf_op jit(solution)/shard_map/all_gather | solution.py:98
  409.1 4.9 fusion.6
  414.0 0.7 gather_fusion.2
  414.8 0.5 stack.8
  415.3 59.6 %all_to_all.26 = f32[128,128,64]{1,2,0:T(8,128)S(1)} all-to-all(f32[128,128,64]{1,2,0:T(8,128)S(1)} %stack.8), channel_id=1, replica_groups=mesh['role'=2,'grp'=64] {'role','grp'}, dimensions={0} | all-to-all | bytes 8388608 | tf_op jit(solution)/shard_map/all_to_all | solution.py:13
  474.9 1.1 fusion.4
  476.0 3.5 fusion.1
  479.6 1.9 fusion.34
  481.5 14.5 %fusion.13 = f32[128,8192]{0,1:T(8,128)} fusion(bf16[416,8192]{1,0:T(8,128)(2,1)} %param.18, bf16[416,8192]{1,0:T(8,128)(2,1)} %param.17, bf16[128,8192]{0,1:T(8,128)(2,1)S(1)} %fusion.1, f32[128,416]{0,1:T(8,128)S(1)} %fusion.34), kind=kOutput, calls=%fused_computation.25 | convolution fusion | flops 1745149952 | bytes 20135936 | tf_op jit(solution)/shard_map/dot_general | solution.py:104
  496.0 661.4 %reduce-scatter.2.cloned.1.call-done = f32[128,64]{0,1:T(8,128)} async-done(((f32[128,8192]{0,1:T(8,128)}), f32[128,64]{0,1:T(8,128)}) %reduce-scatter.2.cloned.1.call-update) | async-done | bytes 32784 | tf_op jit(solution)/shard_map/reduce_scatter | solution.py:105
  1157.5 1.4 add.63
  (52 shorter events, 2.4 us)
Async XLA Ops:
  6.5 187.2 %copy-start = (bf16[72,8192]{1,0:T(8,128)(2,1)S(1)}, bf16[72,8192]{1,0:T(8,128)(2,1)}, u32[]{:S(2)}) copy-start(bf16[72,8192]{1,0:T(8,128)(2,1)} %param.14) | copy-start | bytes 3538948
  9.9 10.8 copy-start.6
  9.9 11.1 copy-start.7
  9.9 12.0 %copy-start.8 = (s32[128]{0:T(128)S(1)}, s32[128]{0:T(128)}, u32[]{:S(2)}) copy-start(s32[128]{0:T(128)} %param.21) | copy-start | bytes 1540
  9.9 12.1 %copy-start.1 = (s32[128]{0:T(128)S(1)}, s32[128]{0:T(128)}, u32[]{:S(2)}) copy-start(s32[128]{0:T(128)} %param.20) | copy-start | bytes 1540
  9.9 62.5 %all-to-all-start = ((f32[128,128,64]{1,2,0:T(8,128)}), f32[128,128,64]{1,2,0:T(8,128)}, u32[]{:S(2)}, u32[]{:S(2)}) async-start(f32[128,128,64]{1,2,0:T(8,128)} %stack.6), calls=%async_computation | async-start | bytes 8388608 | tf_op jit(solution)/shard_map/all_to_all | solution.py:13
  20.6 170.2 %all-reduce.5.cloned.1.call-start = ((), (), s32[]{:S(2)}) async-start(), calls=%async_computation.6 | async-start | bytes 131072
  21.0 0.6 copy-start.4
  21.3 0.6 copy-start.3
  195.7 16.6 %all-to-all-start.1 = ((bf16[128,1,72]{2,1,0:T(2,128)(2,1)}), bf16[128,1,72]{2,1,0:T(2,128)(2,1)S(1)}, u32[]{:S(2)}, u32[]{:S(2)}) async-start(bf16[128,1,72]{2,1,0:T(2,128)(2,1)} %copy.26), calls=%async_computation.1 | async-start | bytes 131072 | tf_op jit(solution)/shard_map/all_to_all | solution.py:69
  203.9 205.2 %all-gather.3.cloned.1.call-start = ((), (), s32[]{:S(2)}) async-start(), calls=%async_computation.5 | async-start | bytes 4227072 | tf_op jit(solution)/shard_map/all_gather | solution.py:98
  206.7 208.0 %copy-start.2 = (f32[128,64]{0,1:T(8,128)S(1)}, f32[128,64]{0,1:T(8,128)}, u32[]{:S(2)}) copy-start(f32[128,64]{0,1:T(8,128)} %param.11) | copy-start | bytes 98308
  214.5 942.9 %reduce-scatter.2.cloned.1.call-start = ((), (), s32[]{:S(2)}) async-start(), calls=%async_computation.4 | async-start | bytes 4227072 | tf_op jit(solution)/shard_map/reduce_scatter | solution.py:105
  415.3 64.3 %slice-start = ((s8[6815744]{0:T(1024)(128)(4,1)}), s8[2621440]{0:T(1024)(128)(4,1)S(1)}, s32[]{:S(2)}) async-start(s8[6815744]{0:T(1024)(128)(4,1)} %bitcast.58), calls=%async_computation.7 | async-start | bytes 5242880
  474.9 1.1 copy-start.5
  474.9 4.6 slice-start.1
Sparse Core Ops, SparseCore 0:
  26.5 164.2 all-reduce.4
  214.6 194.4 all-gather.2
  496.1 661.2 reduce-scatter.1
